TPU v7x, 32 devices: a whole 2x2x4 slice. The times are simulated.
32 devices in a mesh: dom: 8 (over z, y), tile: 4 (over x, core).
Axes of the slice: x: 2, y: 2, z: 4, core: 2. Of those that a mesh axis runs over, the one named last changes fastest.
Arguments:
- embeddings: float32 [2048, 256], P(('dom', 'tile')), may hold values from -1.5 to 1.5
- adagrad_state: float32 [2048], P(('dom', 'tile')), may hold values from 0.1 to 2
- offsets: int32 [2], replicated, may hold values from 1 to 7, as said below
- lhs_rows: int32 [8, 2, 96, 128], P('dom', None, 'tile'), may hold values from 0 to 255
- rhs_rows: int32 [8, 2, 96, 128], P('dom', None, 'tile'), may hold values from 0 to 255
- neg_blocks: int32 [8, 2, 96], P('dom', None, 'tile'), may hold values from 0 to 1
- tile_counts: int32 [8, 2], P('dom'), may hold values from 12 to 72, as said below
Outputs:
- new_embeddings: float32 [2048, 256], P(('dom', 'tile'))
- new_state: float32 [2048], P(('dom', 'tile'))
Inputs may be any that keep to these rules, and one draw needn't show every extreme that they name: `offsets`: in one round of every draw the offset has all bits of a partition number set. `tile_counts`: in every round some bucket has exactly 72 live tiles.
All inputs are finite; a program needn't handle non-finite values.
Results may differ from a plain program's by a relative error of at most 0.007.
Values may be sent and summed in bfloat16 or wider, within the bound.
A program may use at most 64 MiB of HBM per device.

v0:
```python
import jax
import jax.numpy as jnp
from jax import lax
from jax.sharding import PartitionSpec as P

ROUNDS = 2
TURN_TILES = 4


LEARN_RATE = 0.5


def from_partner(block, axis, bit):
    count = lax.axis_size(axis)
    route = []
    for low in range(count):
        high = low | 1 << bit
        if high != low and high < count:
            route += [(low, high), (high, low)]
    return lax.ppermute(block, axis, route)


def shards(embeddings, adagrad_state, offsets, lhs_rows, rhs_rows, neg_blocks, tile_counts):
    tiles_count = lax.axis_size("tile")
    tile_place = lax.axis_index("tile")
    bit_count = lax.axis_size("dom").bit_length() - 1
    quarter, width = embeddings.shape
    rows_all = quarter * tiles_count
    edges = lhs_rows.shape[3]
    slots = lhs_rows.shape[2]
    lhs_local = lhs_rows[0]
    rhs_local = rhs_rows[0]
    neg_local = neg_blocks[0]
    counts = tile_counts[0]
    live_all = jnp.clip(counts - tile_place * slots, 0, slots)
    spread = jnp.arange(edges, dtype=jnp.int32)
    positive = jnp.arange(2 * edges, dtype=jnp.int32)[None, :] == spread[:, None]
    row_ids = jnp.arange(rows_all, dtype=jnp.int32)
    table = embeddings
    state = adagrad_state
    for rnd in range(ROUNDS):
        offset = offsets[rnd]
        low = table.astype(jnp.bfloat16)
        own_block = lax.all_gather(low, "tile", axis=0, tiled=True)
        partner_block = own_block
        for bit in range(bit_count):
            other = from_partner(partner_block, "dom", bit)
            partner_block = jnp.where(offset >> bit & 1 == 1, other, partner_block)
        lhs_round = lhs_local[rnd]
        rhs_round = rhs_local[rnd]
        neg_round = neg_local[rnd]
        live = live_all[rnd]

        def turn(step, accums):
            own_acc, partner_acc = accums
            first = step * TURN_TILES
            lhs_turn = lax.dynamic_slice_in_dim(lhs_round, first, TURN_TILES, 0)
            rhs_turn = lax.dynamic_slice_in_dim(rhs_round, first, TURN_TILES, 0)
            neg_turn = lax.dynamic_slice_in_dim(neg_round, first, TURN_TILES, 0)
            targets = jnp.concatenate(
                [rhs_turn, neg_turn[:, None] * edges + spread[None, :]], axis=1
            )
            pick_left = lhs_turn[:, :, None] == row_ids[None, None, :]
            pick_right = targets[:, :, None] == row_ids[None, None, :]
            left = jnp.einsum(
                "gir,rd->gid",
                pick_left.astype(jnp.bfloat16),
                own_block,
                preferred_element_type=jnp.float32,
            ).astype(jnp.bfloat16)
            right = jnp.einsum(
                "gjr,rd->gjd",
                pick_right.astype(jnp.bfloat16),
                partner_block,
                preferred_element_type=jnp.float32,
            ).astype(jnp.bfloat16)
            scores = jnp.einsum("gid,gjd->gij", left, right, preferred_element_type=jnp.float32)
            coef = jnp.where(
                positive[None], -jax.nn.sigmoid(-scores), jax.nn.sigmoid(scores) / (2 * edges - 1)
            )
            active = first + jnp.arange(TURN_TILES, dtype=jnp.int32) < live
            coef = jnp.where(active[:, None, None], coef, 0.0).astype(jnp.bfloat16)
            grad_left = jnp.einsum("gij,gjd->gid", coef, right, preferred_element_type=jnp.float32)
            grad_right = jnp.einsum("gij,gid->gjd", coef, left, preferred_element_type=jnp.float32)
            own_acc = own_acc + jnp.einsum(
                "gir,gid->rd",
                pick_left.astype(jnp.float32),
                grad_left,
                precision=lax.Precision.HIGHEST,
            )
            partner_acc = partner_acc + jnp.einsum(
                "gjr,gjd->rd",
                pick_right.astype(jnp.float32),
                grad_right,
                precision=lax.Precision.HIGHEST,
            )
            return (own_acc, partner_acc)

        turns = (live + TURN_TILES - 1) // TURN_TILES
        blank = jnp.zeros((rows_all, width), jnp.float32)
        own_acc, partner_acc = lax.fori_loop(0, turns, turn, (blank, blank))
        own_share, partner_share = (
            lax.psum_scatter(own_acc, "tile", scatter_dimension=0, tiled=True),
            lax.psum_scatter(partner_acc, "tile", scatter_dimension=0, tiled=True),
        )
        returned = partner_share
        for bit in range(bit_count):
            other = from_partner(returned, "dom", bit)
            returned = jnp.where(offset >> bit & 1 == 1, other, returned)
        total = own_share + returned
        state = state + jnp.mean(total * total, axis=1)
        table = table - LEARN_RATE * total / jnp.sqrt(state)[:, None]
    return (table, state)


def solution(mesh):
    return jax.shard_map(
        shards,
        mesh=mesh,
        in_specs=(
            P(("dom", "tile"), None),
            P(("dom", "tile")),
            P(),
            P("dom", None, "tile", None),
            P("dom", None, "tile", None),
            P("dom", None, "tile"),
            P("dom", None),
        ),
        out_specs=(P(("dom", "tile"), None), P(("dom", "tile"))),
        check_vma=False,
    )
```

profile of v0, /device:TPU:0, one launch (start us, length us, event | category | flops | bytes accessed | tf_op | source)
XLA Modules:
  0.0 206.7 jit_solution(8559124530304760470)
XLA Ops:
  8.1 6.5 %all_gather.6 = bf16[256,256]{1,0:T(8,128)(2,1)S(1)} all-gather(bf16[64,256]{1,0:T(8,128)(2,1)S(1)} %convert_element_type.32), channel_id=1, replica_groups=mesh['dom'=8,'tile'=4] {'tile'}, dimensions={0}, use_global_device_ids=true | all-gather | bytes 163840 | tf_op jit(solution)/shard_map/all_gather | solution.py:44
  14.5 1.9 collective-permute-start
  21.6 1.6 collective-permute-start.1
  23.2 3.9 %collective-permute-done.1 = bf16[256,256]{1,0:T(8,128)(2,1)S(1)} collective-permute-done((bf16[256,256]{1,0:T(8,128)(2,1)S(1)}, bf16[256,256]{1,0:T(8,128)(2,1)S(1)}, u32[]{:S(2)}, u32[]{:S(2)}) %collective-permute-start.1) | collective-permute-done | bytes 131104 | tf_op jit(solution)/shard_map/ppermute | solution.py:20
  27.1 2.7 %collective-permute-start.2 = (bf16[256,256]{1,0:T(8,128)(2,1)S(1)}, bf16[256,256]{1,0:T(8,128)(2,1)S(1)}, u32[]{:S(2)}, u32[]{:S(2)}) collective-permute-start(bf16[256,256]{1,0:T(8,128)(2,1)S(1)} %broadcast_select_fusion.4), channel_id=1, source_target_pairs={{0,16},{16,0},{4,20},{20,4},{8,24},{24,8},{12,28},{28,12},{1,17},{... | collective-permute-start | bytes 393224 | tf_op jit(solution)/shard_map/ppermute | solution.py:20
  29.8 5.7 %collective-permute-done.2 = bf16[256,256]{1,0:T(8,128)(2,1)S(1)} collective-permute-done((bf16[256,256]{1,0:T(8,128)(2,1)S(1)}, bf16[256,256]{1,0:T(8,128)(2,1)S(1)}, u32[]{:S(2)}, u32[]{:S(2)}) %collective-permute-start.2) | collective-permute-done | bytes 131104 | tf_op jit(solution)/shard_map/ppermute | solution.py:20
  35.6 25.3 %while.28 = (s32[]{:T(128)}, f32[256,256]{1,0:T(8,128)S(1)}, f32[256,256]{1,0:T(8,128)S(1)}, s32[]{:T(128)}, s32[24,128]{1,0:T(8,128)S(1)}, /*index=5*/s32[]{:T(...) while((s32[]{:T(128)}, f32[256,256]{1,0:T(8,128)S(1)}, ...), condition=%wide.region_1.2_spmd.clone.clone, body=%wide.region_0.1_spmd.clone.clone.sunk | while | flops 1613268480 | bytes 7698683 | solution.py:101
  61.7 19.2 %reduce-scatter.7.cloned.1.call-done = f32[64,256]{1,0:T(8,128)} async-done(((f32[256,256]{1,0:T(8,128)}), f32[64,256]{1,0:T(8,128)}) %reduce-scatter.7.cloned.1.call-update) | async-done | bytes 65552 | tf_op jit(solution)/shard_map/reduce_scatter | solution.py:104
  82.4 2.9 %collective-permute-done.3 = f32[64,256]{1,0:T(8,128)S(1)} collective-permute-done((f32[64,256]{1,0:T(8,128)}, f32[64,256]{1,0:T(8,128)S(1)}, u32[]{:S(2)}, u32[]{:S(2)}) %collective-permute-start.3) | collective-permute-done | bytes 65568 | tf_op jit(solution)/shard_map/ppermute | solution.py:20
  85.4 1.6 collective-permute-start.4
  86.9 2.8 %collective-permute-done.4 = f32[64,256]{1,0:T(8,128)S(1)} collective-permute-done((f32[64,256]{1,0:T(8,128)S(1)}, f32[64,256]{1,0:T(8,128)S(1)}, u32[]{:S(2)}, u32[]{:S(2)}) %collective-permute-start.4) | collective-permute-done | bytes 65568 | tf_op jit(solution)/shard_map/ppermute | solution.py:20
  89.7 2.5 %collective-permute-start.5 = (f32[64,256]{1,0:T(8,128)S(1)}, f32[64,256]{1,0:T(8,128)S(1)}, u32[]{:S(2)}, u32[]{:S(2)}) collective-permute-start(f32[64,256]{1,0:T(8,128)S(1)} %broadcast_select_fusion.9), channel_id=1, source_target_pairs={{0,16},{16,0},{4,20},{20,4},{8,24},{24,8},{12,28},{28,12},{1,17},{... | collective-permute-start | bytes 196616 | tf_op jit(solution)/shard_map/ppermute | solution.py:20
  92.2 11.4 %reduce-scatter.5.cloned.1.call-done = f32[64,256]{1,0:T(8,128)} async-done(((f32[256,256]{1,0:T(8,128)}), f32[64,256]{1,0:T(8,128)}) %reduce-scatter.5.cloned.1.call-update) | async-done | bytes 65552 | tf_op jit(solution)/shard_map/reduce_scatter | solution.py:103
  105.3 5.4 %all_gather.7 = bf16[256,256]{1,0:T(8,128)(2,1)S(1)} all-gather(bf16[64,256]{1,0:T(8,128)(2,1)S(1)} %fusion.29), channel_id=1, replica_groups=mesh['dom'=8,'tile'=4] {'tile'}, dimensions={0}, use_global_device_ids=true | all-gather | bytes 163840 | tf_op jit(solution)/shard_map/all_gather | solution.py:44
  112.8 3.6 %collective-permute-done.6 = bf16[256,256]{1,0:T(8,128)(2,1)S(1)} collective-permute-done((bf16[256,256]{1,0:T(8,128)(2,1)S(1)}, bf16[256,256]{1,0:T(8,128)(2,1)S(1)}, u32[]{:S(2)}, u32[]{:S(2)}) %collective-permute-start.6) | collective-permute-done | bytes 131104 | tf_op jit(solution)/shard_map/ppermute | solution.py:20
  118.7 2.9 %collective-permute-done.7 = bf16[256,256]{1,0:T(8,128)(2,1)S(1)} collective-permute-done((bf16[256,256]{1,0:T(8,128)(2,1)S(1)}, bf16[256,256]{1,0:T(8,128)(2,1)S(1)}, u32[]{:S(2)}, u32[]{:S(2)}) %collective-permute-start.7) | collective-permute-done | bytes 131104 | tf_op jit(solution)/shard_map/ppermute | solution.py:20
  121.5 2.5 %collective-permute-start.8 = (bf16[256,256]{1,0:T(8,128)(2,1)S(1)}, bf16[256,256]{1,0:T(8,128)(2,1)S(1)}, u32[]{:S(2)}, u32[]{:S(2)}) collective-permute-start(bf16[256,256]{1,0:T(8,128)(2,1)S(1)} %broadcast_select_fusion.1), channel_id=1, source_target_pairs={{0,16},{16,0},{4,20},{20,4},{8,24},{24,8},{12,28},{28,12},{1,17},{... | collective-permute-start | bytes 393224 | tf_op jit(solution)/shard_map/ppermute | solution.py:20
  125.3 3.8 %collective-permute-done.8 = bf16[256,256]{1,0:T(8,128)(2,1)S(1)} collective-permute-done((bf16[256,256]{1,0:T(8,128)(2,1)S(1)}, bf16[256,256]{1,0:T(8,128)(2,1)S(1)}, u32[]{:S(2)}, u32[]{:S(2)}) %collective-permute-start.8) | collective-permute-done | bytes 131104 | tf_op jit(solution)/shard_map/ppermute | solution.py:20
  129.2 25.3 %while.29 = (s32[]{:T(128)}, f32[256,256]{1,0:T(8,128)S(1)}, f32[256,256]{1,0:T(8,128)S(1)}, s32[]{:T(128)}, s32[24,128]{1,0:T(8,128)S(1)}, /*index=5*/s32[]{:T(...) while((s32[]{:T(128)}, f32[256,256]{1,0:T(8,128)S(1)}, ...), condition=%wide.region_6.7_spmd.clone.clone, body=%wide.region_5.6_spmd.clone.clone.sunk | while | flops 1613268480 | bytes 7698683 | solution.py:101
  155.3 20.1 %reduce-scatter.11.cloned.1.call-done = f32[64,256]{1,0:T(8,128)} async-done(((f32[256,256]{1,0:T(8,128)}), f32[64,256]{1,0:T(8,128)}) %reduce-scatter.11.cloned.1.call-update) | async-done | bytes 65552 | tf_op jit(solution)/shard_map/reduce_scatter | solution.py:104
  176.9 3.0 %collective-permute-done.9 = f32[64,256]{1,0:T(8,128)S(1)} collective-permute-done((f32[64,256]{1,0:T(8,128)}, f32[64,256]{1,0:T(8,128)S(1)}, u32[]{:S(2)}, u32[]{:S(2)}) %collective-permute-start.9) | collective-permute-done | bytes 65568 | tf_op jit(solution)/shard_map/ppermute | solution.py:20
  181.5 2.8 %collective-permute-done.10 = f32[64,256]{1,0:T(8,128)S(1)} collective-permute-done((f32[64,256]{1,0:T(8,128)S(1)}, f32[64,256]{1,0:T(8,128)S(1)}, u32[]{:S(2)}, u32[]{:S(2)}) %collective-permute-start.10) | collective-permute-done | bytes 65568 | tf_op jit(solution)/shard_map/ppermute | solution.py:20
  184.2 2.5 %collective-permute-start.11 = (f32[64,256]{1,0:T(8,128)S(1)}, f32[64,256]{1,0:T(8,128)S(1)}, u32[]{:S(2)}, u32[]{:S(2)}) collective-permute-start(f32[64,256]{1,0:T(8,128)S(1)} %broadcast_select_fusion.7), channel_id=1, source_target_pairs={{0,16},{16,0},{4,20},{20,4},{8,24},{24,8},{12,28},{28,12},{1,17},{... | collective-permute-start | bytes 196616 | tf_op jit(solution)/shard_map/ppermute | solution.py:20
  186.7 11.2 %reduce-scatter.9.cloned.1.call-done = f32[64,256]{1,0:T(8,128)} async-done(((f32[256,256]{1,0:T(8,128)}), f32[64,256]{1,0:T(8,128)}) %reduce-scatter.9.cloned.1.call-update) | async-done | bytes 65552 | tf_op jit(solution)/shard_map/reduce_scatter | solution.py:103
  (224 shorter events, 66.4 us)
Async XLA Ops:
  7.2 73.7 %reduce-scatter.7.cloned.1.call-start = ((), (), s32[]{:S(2)}) async-start(), calls=%async_computation.5 | async-start | bytes 327680 | tf_op jit(solution)/shard_map/reduce_scatter | solution.py:104
  14.5 7.0 %collective-permute-start = (bf16[256,256]{1,0:T(8,128)(2,1)S(1)}, bf16[256,256]{1,0:T(8,128)(2,1)S(1)}, u32[]{:S(2)}, u32[]{:S(2)}) collective-permute-start(bf16[256,256]{1,0:T(8,128)(2,1)S(1)} %all_gather.6), channel_id=1, source_target_pairs={{0,4},{4,0},{8,12},{12,8},{16,20},{20,16},{24,28},{28,24},{1,5},{5... | collective-permute-start | bytes 393224 | tf_op jit(solution)/shard_map/ppermute | solution.py:20
  21.5 1.7 copy-start.7
  21.5 1.7 copy-start.8
  21.6 5.5 %collective-permute-start.1 = (bf16[256,256]{1,0:T(8,128)(2,1)S(1)}, bf16[256,256]{1,0:T(8,128)(2,1)S(1)}, u32[]{:S(2)}, u32[]{:S(2)}) collective-permute-start(bf16[256,256]{1,0:T(8,128)(2,1)S(1)} %broadcast_select_fusion.3), channel_id=1, source_target_pairs={{0,8},{8,0},{4,12},{12,4},{16,24},{24,16},{20,28},{28,20},{1,9},{9... | collective-permute-start | bytes 393224 | tf_op jit(solution)/shard_map/ppermute | solution.py:20
  27.1 2.7 %copy-start.10 = (s32[1,2,24]{2,1,0:T(2,128)S(1)}, s32[1,2,24]{2,1,0:T(2,128)}, u32[]{:S(2)}) copy-start(s32[1,2,24]{2,1,0:T(2,128)} %param.16) | copy-start | bytes 580
  27.1 8.4 %collective-permute-start.2 = (bf16[256,256]{1,0:T(8,128)(2,1)S(1)}, bf16[256,256]{1,0:T(8,128)(2,1)S(1)}, u32[]{:S(2)}, u32[]{:S(2)}) collective-permute-start(bf16[256,256]{1,0:T(8,128)(2,1)S(1)} %broadcast_select_fusion.4), channel_id=1, source_target_pairs={{0,16},{16,0},{4,20},{20,4},{8,24},{24,8},{12,28},{28,12},{1,17},{... | collective-permute-start | bytes 393224 | tf_op jit(solution)/shard_map/ppermute | solution.py:20
  60.9 21.4 %copy-start.3 = (f32[256,256]{1,0:T(8,128)}, f32[256,256]{1,0:T(8,128)S(1)}, u32[]{:S(2)}) copy-start(f32[256,256]{1,0:T(8,128)S(1)} %get-tuple-element.146) | copy-start | bytes 786436
  61.6 41.9 %reduce-scatter.5.cloned.1.call-start = ((), (), s32[]{:S(2)}) async-start(), calls=%async_computation.4 | async-start | bytes 327680 | tf_op jit(solution)/shard_map/reduce_scatter | solution.py:103
  80.9 4.5 %collective-permute-start.3 = (f32[64,256]{1,0:T(8,128)}, f32[64,256]{1,0:T(8,128)S(1)}, u32[]{:S(2)}, u32[]{:S(2)}) collective-permute-start(f32[64,256]{1,0:T(8,128)} %reduce-scatter.7.cloned.1.call-done), channel_id=1, source_target_pairs={{0,4},{4,0},{8,12},{12,8},{16,20},{20,16},{24,28},{28,24},{1,5},{5... | collective-permute-start | bytes 196616 | tf_op jit(solution)/shard_map/ppermute | solution.py:20
  82.3 3.0 %copy-start.5 = (f32[64,256]{1,0:T(8,128)S(1)}, f32[64,256]{1,0:T(8,128)}, u32[]{:S(2)}) copy-start(f32[64,256]{1,0:T(8,128)} %reduce-scatter.7.cloned.1.call-done) | copy-start | bytes 196612
  82.4 93.0 %reduce-scatter.11.cloned.1.call-start = ((), (), s32[]{:S(2)}) async-start(), calls=%async_computation.7 | async-start | bytes 327680 | tf_op jit(solution)/shard_map/reduce_scatter | solution.py:104
  85.4 4.3 %collective-permute-start.4 = (f32[64,256]{1,0:T(8,128)S(1)}, f32[64,256]{1,0:T(8,128)S(1)}, u32[]{:S(2)}, u32[]{:S(2)}) collective-permute-start(f32[64,256]{1,0:T(8,128)S(1)} %broadcast_select_fusion.8), channel_id=1, source_target_pairs={{0,8},{8,0},{4,12},{12,4},{16,24},{24,16},{20,28},{28,20},{1,9},{9... | collective-permute-start | bytes 196616 | tf_op jit(solution)/shard_map/ppermute | solution.py:20
  89.7 15.5 %copy-start.4 = (f32[64,256]{1,0:T(8,128)S(1)}, f32[64,256]{1,0:T(8,128)}, u32[]{:S(2)}) copy-start(f32[64,256]{1,0:T(8,128)} %param.11) | copy-start | bytes 196612
  89.7 13.9 %collective-permute-start.5 = (f32[64,256]{1,0:T(8,128)S(1)}, f32[64,256]{1,0:T(8,128)S(1)}, u32[]{:S(2)}, u32[]{:S(2)}) collective-permute-start(f32[64,256]{1,0:T(8,128)S(1)} %broadcast_select_fusion.9), channel_id=1, source_target_pairs={{0,16},{16,0},{4,20},{20,4},{8,24},{24,8},{12,28},{28,12},{1,17},{... | collective-permute-start | bytes 196616 | tf_op jit(solution)/shard_map/ppermute | solution.py:20
  110.7 5.7 %collective-permute-start.6 = (bf16[256,256]{1,0:T(8,128)(2,1)S(1)}, bf16[256,256]{1,0:T(8,128)(2,1)S(1)}, u32[]{:S(2)}, u32[]{:S(2)}) collective-permute-start(bf16[256,256]{1,0:T(8,128)(2,1)S(1)} %all_gather.7), channel_id=1, source_target_pairs={{0,4},{4,0},{8,12},{12,8},{16,20},{20,16},{24,28},{28,24},{1,5},{5... | collective-permute-start | bytes 393224 | tf_op jit(solution)/shard_map/ppermute | solution.py:20
  116.5 5.0 %collective-permute-start.7 = (bf16[256,256]{1,0:T(8,128)(2,1)S(1)}, bf16[256,256]{1,0:T(8,128)(2,1)S(1)}, u32[]{:S(2)}, u32[]{:S(2)}) collective-permute-start(bf16[256,256]{1,0:T(8,128)(2,1)S(1)} %broadcast_select_fusion), channel_id=1, source_target_pairs={{0,8},{8,0},{4,12},{12,4},{16,24},{24,16},{20,28},{28,20},{1,9},{9... | collective-permute-start | bytes 393224 | tf_op jit(solution)/shard_map/ppermute | solution.py:20
  121.5 7.6 %collective-permute-start.8 = (bf16[256,256]{1,0:T(8,128)(2,1)S(1)}, bf16[256,256]{1,0:T(8,128)(2,1)S(1)}, u32[]{:S(2)}, u32[]{:S(2)}) collective-permute-start(bf16[256,256]{1,0:T(8,128)(2,1)S(1)} %broadcast_select_fusion.1), channel_id=1, source_target_pairs={{0,16},{16,0},{4,20},{20,4},{8,24},{24,8},{12,28},{28,12},{1,17},{... | collective-permute-start | bytes 393224 | tf_op jit(solution)/shard_map/ppermute | solution.py:20
  154.5 22.4 %copy-start.1 = (f32[256,256]{1,0:T(8,128)}, f32[256,256]{1,0:T(8,128)S(1)}, u32[]{:S(2)}) copy-start(f32[256,256]{1,0:T(8,128)S(1)} %get-tuple-element.148) | copy-start | bytes 786436
  155.2 42.7 %reduce-scatter.9.cloned.1.call-start = ((), (), s32[]{:S(2)}) async-start(), calls=%async_computation.6 | async-start | bytes 327680 | tf_op jit(solution)/shard_map/reduce_scatter | solution.py:103
  175.4 4.5 %collective-permute-start.9 = (f32[64,256]{1,0:T(8,128)}, f32[64,256]{1,0:T(8,128)S(1)}, u32[]{:S(2)}, u32[]{:S(2)}) collective-permute-start(f32[64,256]{1,0:T(8,128)} %reduce-scatter.11.cloned.1.call-done), channel_id=1, source_target_pairs={{0,4},{4,0},{8,12},{12,8},{16,20},{20,16},{24,28},{28,24},{1,5},{5... | collective-permute-start | bytes 196616 | tf_op jit(solution)/shard_map/ppermute | solution.py:20
  176.9 3.0 %copy-start.6 = (f32[64,256]{1,0:T(8,128)S(1)}, f32[64,256]{1,0:T(8,128)}, u32[]{:S(2)}) copy-start(f32[64,256]{1,0:T(8,128)} %reduce-scatter.11.cloned.1.call-done) | copy-start | bytes 196612
  179.9 4.3 %collective-permute-start.10 = (f32[64,256]{1,0:T(8,128)S(1)}, f32[64,256]{1,0:T(8,128)S(1)}, u32[]{:S(2)}, u32[]{:S(2)}) collective-permute-start(f32[64,256]{1,0:T(8,128)S(1)} %broadcast_select_fusion.6), channel_id=1, source_target_pairs={{0,8},{8,0},{4,12},{12,4},{16,24},{24,16},{20,28},{28,20},{1,9},{9... | collective-permute-start | bytes 196616 | tf_op jit(solution)/shard_map/ppermute | solution.py:20
  184.2 13.7 %collective-permute-start.11 = (f32[64,256]{1,0:T(8,128)S(1)}, f32[64,256]{1,0:T(8,128)S(1)}, u32[]{:S(2)}, u32[]{:S(2)}) collective-permute-start(f32[64,256]{1,0:T(8,128)S(1)} %broadcast_select_fusion.7), channel_id=1, source_target_pairs={{0,16},{16,0},{4,20},{20,4},{8,24},{24,8},{12,28},{28,12},{1,17},{... | collective-permute-start | bytes 196616 | tf_op jit(solution)/shard_map/ppermute | solution.py:20
  (5 other events, 3.4 us)
Sparse Core Ops, SparseCore 0:
  61.8 19.0 reduce-scatter.6
  83.5 20.0 reduce-scatter.4
  155.4 19.9 reduce-scatter.10
  177.9 20.0 reduce-scatter.8
where the time goes:
time: 207 us
  waiting for transfers between devices  93.2 us (45%)
  matrix products  39.6 us (19%)
  starting transfers between devices  22.9 us (11%)
  between operations  19.1 us (9%)
  other arithmetic  14.2 us (7%)
  blocking collectives  11.9 us (6%)
  local copies, waits for them, and re-layouts  4.79 us (2%)
    reduce_scatter x2, waiting for transfers between devices, shards(): lax.psum_scatter(partner_acc, 'tile', scatter_dimension=0, tiled=True)  39.3 us
    ppermute x12, waiting for transfers between devices, from_partner(): return lax.ppermute(block, axis, route)  31.3 us
    ppermute x12, starting transfers between devices, from_partner(): return lax.ppermute(block, axis, route)  22.7 us
    reduce_scatter x2, waiting for transfers between devices, shards(): lax.psum_scatter(own_acc, 'tile', scatter_dimension=0, tiled=True)  22.6 us
    all_gather x2, blocking collectives, shards(): own_block = lax.all_gather(low, 'tile', axis=0, tiled=True)  11.9 us
    dot_general x12, matrix products, turn(): jnp.einsum('gjr,gjd->rd', pick_right.astype(jnp.float32), grad_right, pre...  10.2 us
    lt x12, other arithmetic, turn(): active = first + jnp.arange(TURN_TILES, dtype=jnp.int32) < live  7.84 us
    dot_general x12, matrix products, turn(): jnp.einsum('gir,gid->rd', pick_left.astype(jnp.float32), grad_left, preci...  6.59 us
  transfers between devices with their start and end apart: 16, of which 13 were waited for; matrix products, arithmetic and copies ran while one was open for 1% of the time, Pallas kernels for 0%

commit v1 on v0

v1 whole, which is shorter than its diff:
```python
import functools

import jax
import jax.numpy as jnp
from jax import lax
from jax.experimental import pallas as pl
from jax.experimental.pallas import tpu as pltpu
from jax.sharding import PartitionSpec as P

ROUNDS = 2
LEARN_RATE = 0.5
MESH = pl.DeviceIdType.MESH
NEG_AT = 24
RHS_AT = 32
MSG = 64
LANES = 128
CHUNK = 8
BF = jnp.bfloat16
F32 = jnp.float32


def nt(a, b):
    return lax.dot_general(a, b, (((1,), (1,)), ((), ())), preferred_element_type=F32)


def tn(a, b):
    return lax.dot_general(a, b, (((0,), (0,)), ((), ())), preferred_element_type=F32)


class Item:
    def __init__(self, refs, fixed, offset, place):
        self.cur, self.recv, self.got, self.ssem, self.rsem, self.gs, self.gr = refs
        self.fixed, self.offset = fixed, offset
        self.dom, self.tile, self.n_dom, self.n_tile = place
        self.stages = 1 if fixed else self.n_dom.bit_length() - 1
        self.at = 0
        self.sends = []

    def start(self):
        if self.fixed:
            to = self.n_dom - 1 - self.dom
        else:
            to = flip_bit(self.dom, self.at)
        self.copy = pltpu.make_async_remote_copy(
            src_ref=self.cur.at[self.at],
            dst_ref=self.recv.at[self.at],
            send_sem=self.ssem.at[self.at],
            recv_sem=self.rsem.at[self.at],
            device_id=(to, self.tile),
            device_id_type=MESH,
        )
        self.copy.start()
        self.sends.append(self.copy)

    def advance(self):
        self.copy.wait_recv()
        if self.fixed:
            final = self.recv.at[0]
        else:
            new = self.recv[self.at].astype(F32)
            old = self.cur[self.at].astype(F32)
            bit = (self.offset >> self.at) & 1
            take = jnp.broadcast_to(bit, new.shape) == 1
            self.cur[self.at + 1] = jnp.where(take, new, old).astype(BF)
            final = self.cur.at[self.at + 1]
        self.at += 1
        if self.at < self.stages:
            self.start()
            return
        self.copies = spread(final, self.got, self.gs, self.gr, self.tile, self.dom, self.n_tile)
        self.sends += self.copies
        self.got[self.tile] = final[...]

    def finish(self):
        while self.at < self.stages:
            self.advance()

    def arrive(self):
        for copy in self.copies:
            copy.wait_recv()


def flip_bit(value, bit):
    step = 1 << bit
    return value + step - 2 * step * lax.rem(lax.div(value, step), 2)


def spread(src, got, send_sems, recv_sems, tile, dom, n_tile):
    copies = []
    for d in range(1, n_tile):
        copy = pltpu.make_async_remote_copy(
            src_ref=src,
            dst_ref=got.at[tile],
            send_sem=send_sems.at[d - 1],
            recv_sem=recv_sems.at[d - 1],
            device_id=(dom, lax.rem(tile + d, n_tile)),
            device_id_type=MESH,
        )
        copy.start()
        copies.append(copy)
    return copies


def kernel(direct0, n_dom, n_tile, senders, edges, *refs):
    offs, counts, neg, emb, state, lhs, rhs, out, out_state = refs[:9]
    items = [refs[9 + 7 * i : 16 + 7 * i] for i in range(4)]
    own_got, own_gs, own_gr, group, acc, own_cur = refs[37:]
    dom, tile = lax.axis_index("dom"), lax.axis_index("tile")
    quarter, width = emb.shape
    rows_all = quarter * n_tile
    slots = lhs.shape[1]
    bits = n_dom.bit_length() - 1

    barrier = pltpu.get_barrier_semaphore()
    peers = [(dom, lax.rem(tile + d, n_tile)) for d in range(1, n_tile)]
    peers += [(flip_bit(dom, bit), tile) for bit in range(bits)]
    peers += [(n_dom - 1 - dom, tile)]
    for peer in peers:
        pl.semaphore_signal(barrier, inc=1, device_id=peer, device_id_type=MESH)

    place = (dom, tile, n_dom, n_tile)
    table0 = Item(items[0], direct0, offs[0], place)
    rows0 = Item(items[1], direct0, offs[0], place)
    rows1 = Item(items[2], not direct0, offs[1], place)
    table1 = Item(items[3], not direct0, offs[1], place)

    lane = lax.broadcasted_iota(jnp.int32, (1, LANES), 1)
    slot_of = lax.broadcasted_iota(jnp.int32, (slots, edges), 0) + tile * slots
    low = emb[...].astype(BF)
    table0.cur[0] = low
    for rnd in range(ROUNDS):
        alive = slot_of < jnp.broadcast_to(counts[rnd], slot_of.shape)
        left = jnp.where(alive, lhs[rnd].astype(F32), -1.0)
        right = jnp.where(alive, rhs[rnd].astype(F32), -1.0)
        blocks = jnp.zeros((1, LANES), F32)
        for g in range(slots):
            value = jnp.broadcast_to(neg[rnd, g], blocks.shape).astype(F32)
            blocks = jnp.where(lane == tile * slots + g, value, blocks)
        pad = jnp.zeros((RHS_AT - slots, LANES), F32)
        first = lax.broadcasted_iota(jnp.int32, pad.shape, 0) == NEG_AT - slots
        packed = jnp.concatenate([left, jnp.where(first, blocks, 0.0), right, pad], axis=0)
        packed = packed.astype(BF)
        own_cur[rnd] = packed
        own_got[rnd, tile] = packed
        (rows0 if rnd == 0 else rows1).cur[0] = packed

    pl.semaphore_wait(barrier, len(peers))

    table0.start()
    rows0.start()
    own = [
        spread(own_cur.at[rnd], own_got.at[rnd], own_gs.at[rnd], own_gr.at[rnd], tile, dom, n_tile)
        for rnd in range(ROUNDS)
    ]
    rows1.start()

    chunks = slots // CHUNK
    span = CHUNK * edges
    slot_row = lax.broadcasted_iota(jnp.int32, (LANES, span), 0)
    edge_slot = lax.broadcasted_iota(jnp.int32, (LANES, span), 1) // edges

    def fill(i, carry):
        group[i] = jnp.where(slot_row == edge_slot + i * CHUNK, 1.0, 0.0).astype(BF)
        return carry

    lax.fori_loop(0, senders * chunks, fill, 0)

    key = lax.broadcasted_iota(jnp.int32, (rows_all, edges), 0).astype(F32)
    mine = (lax.broadcasted_iota(jnp.int32, (quarter, edges), 0) + tile * quarter).astype(F32)

    def count(which, got, swap):
        acc[which] = jnp.zeros(acc.shape[1:], F32)

        def body(s, carry):
            held = got[s].astype(F32)
            for chunk in range(chunks):
                keys, mines = [], []
                for g in range(chunk * CHUNK, (chunk + 1) * CHUNK):
                    src = held[g : g + 1]
                    dst = held[RHS_AT + g : RHS_AT + g + 1]
                    for_mine, for_key = (dst, src) if swap else (src, dst)
                    keys.append(jnp.where(key == for_key, 1.0, 0.0).astype(BF))
                    mines.append(jnp.where(mine == for_mine, 1.0, 0.0).astype(BF))
                pick_mine = jnp.concatenate(mines, axis=1)
                pick = jnp.concatenate([jnp.concatenate(keys, axis=1), pick_mine], axis=0)
                against = jnp.concatenate([group[s * chunks + chunk], pick_mine], axis=0)
                acc[which] += nt(pick, against)
            return carry

        lax.fori_loop(0, senders, body, 0)

    def neg_row(got):
        total = got[0, RHS_AT - 16 : RHS_AT].astype(F32)
        for s in range(1, senders):
            total = total + got[s, RHS_AT - 16 : RHS_AT].astype(F32)
        at = NEG_AT - RHS_AT + 16
        return total[at : at + 1]

    key_block = (lax.broadcasted_iota(jnp.int32, (rows_all, LANES), 0) // edges).astype(F32)
    mine_block = (
        (lax.broadcasted_iota(jnp.int32, (quarter, LANES), 0) + tile * quarter) // edges
    ).astype(F32)

    def pair_counts(rnd, own_rows, other_rows):
        a, b = 2 * rnd, 2 * rnd + 1
        own_key = acc[a, :rows_all, :LANES] + jnp.where(key_block == neg_row(own_rows), 1.0, 0.0)
        own_mine = acc[a, rows_all:, :LANES]
        other_key = acc[b, :rows_all, :LANES]
        other_mine = acc[b, rows_all:, :LANES] + jnp.where(
            mine_block == neg_row(other_rows), 1.0, 0.0
        )
        every = nt(
            jnp.concatenate([own_key, other_key], axis=1).astype(BF),
            jnp.concatenate([own_mine, other_mine], axis=1).astype(BF),
        )
        positive = acc[a, :rows_all, LANES:] + acc[b, :rows_all, LANES:]
        return every - positive, positive

    eye = lax.broadcasted_iota(jnp.int32, (quarter, quarter), 0) == lax.broadcasted_iota(
        jnp.int32, (quarter, quarter), 1
    )

    def update(low, got, pairs, table, held):
        negative, positive = pairs
        other = jnp.concatenate([got[s] for s in range(n_tile)], axis=0)
        scores = nt(other, low)
        off_coef = (jax.nn.sigmoid(scores) / (2 * edges - 1)).astype(BF).astype(F32)
        on_coef = (-jax.nn.sigmoid(-scores)).astype(BF).astype(F32)
        weight = negative * off_coef + positive * on_coef
        high = weight.astype(BF)
        rest = (weight - high.astype(F32)).astype(BF)
        both = tn(jnp.concatenate([high, rest], axis=1), other)
        total = both[:quarter] + both[quarter:]
        held = held + jnp.sum(total * total, axis=1, keepdims=True) / width
        return table - LEARN_RATE * total / jnp.sqrt(held), held

    for copy in own[0]:
        copy.wait_recv()
    count(0, own_got.at[0], False)
    while table0.at < table0.stages:
        table0.advance()
        rows0.advance()
    rows1.advance()
    for copy in own[1]:
        copy.wait_recv()
    count(2, own_got.at[1], False)
    rows1.finish()
    rows0.arrive()
    count(1, rows0.got, True)
    pairs = pair_counts(0, own_got.at[0], rows0.got)
    table0.arrive()
    held = jnp.sum(jnp.where(eye, state[...], 0.0), axis=1, keepdims=True)
    table, held = update(low, table0.got, pairs, emb[...], held)
    low = table.astype(BF)
    table1.cur[0] = low
    out[...] = table
    table1.start()
    rows1.arrive()
    count(3, rows1.got, True)
    pairs = pair_counts(1, own_got.at[1], rows1.got)
    table1.finish()
    table1.arrive()
    table, held = update(table1.cur[0], table1.got, pairs, out[...], held)
    out[...] = table
    out_state[...] = jnp.sum(jnp.where(eye, held, 0.0), axis=0, keepdims=True)
    for copy in table0.sends + rows0.sends + rows1.sends + table1.sends + own[0] + own[1]:
        copy.wait_send()


def shards(n_dom, n_tile, embeddings, adagrad_state, offsets, lhs_rows, rhs_rows, neg_blocks, tile_counts):
    quarter, width = embeddings.shape
    slots, edges = lhs_rows.shape[2], lhs_rows.shape[3]
    rows_all = quarter * n_tile
    bits = n_dom.bit_length() - 1
    senders = (3 * n_tile + 3) // 4
    dma = pltpu.SemaphoreType.DMA

    def item(rows, lanes):
        return [
            pltpu.VMEM((bits + 1, rows, lanes), BF),
            pltpu.VMEM((bits, rows, lanes), BF),
            pltpu.VMEM((n_tile, rows, lanes), BF),
            dma((bits,)),
            dma((bits,)),
            dma((n_tile - 1,)),
            dma((n_tile - 1,)),
        ]

    smem = pl.BlockSpec(memory_space=pltpu.SMEM)
    vmem = pl.BlockSpec(memory_space=pltpu.VMEM)

    def call(direct0, *args):
        return pl.pallas_call(
            functools.partial(kernel, direct0, n_dom, n_tile, senders, edges),
            out_shape=(
                jax.ShapeDtypeStruct((quarter, width), F32),
                jax.ShapeDtypeStruct((1, quarter), F32),
            ),
            in_specs=[smem] * 3 + [vmem] * 4,
            out_specs=(vmem, vmem),
            scratch_shapes=item(quarter, width)
            + item(MSG, LANES)
            + item(MSG, LANES)
            + item(quarter, width)
            + [
                pltpu.VMEM((ROUNDS, n_tile, MSG, LANES), BF),
                dma((ROUNDS, n_tile - 1)),
                dma((ROUNDS, n_tile - 1)),
                pltpu.VMEM((senders * slots // CHUNK, LANES, CHUNK * edges), BF),
                pltpu.VMEM((2 * ROUNDS, rows_all + quarter, LANES + quarter), F32),
                pltpu.VMEM((ROUNDS, MSG, LANES), BF),
            ],
            compiler_params=pltpu.CompilerParams(
                collective_id=0 if direct0 else 1,
                has_side_effects=True,
                vmem_limit_bytes=40 << 20,
            ),
        )(*args)

    table, state = lax.cond(
        offsets[0] == n_dom - 1,
        functools.partial(call, True),
        functools.partial(call, False),
        offsets,
        tile_counts[0],
        neg_blocks[0],
        embeddings,
        adagrad_state.reshape(1, quarter),
        lhs_rows[0],
        rhs_rows[0],
    )
    return table, state.reshape(quarter)


def solution(mesh):
    return jax.shard_map(
        functools.partial(shards, mesh.shape["dom"], mesh.shape["tile"]),
        mesh=mesh,
        in_specs=(
            P(("dom", "tile"), None),
            P(("dom", "tile")),
            P(),
            P("dom", None, "tile", None),
            P("dom", None, "tile", None),
            P("dom", None, "tile"),
            P("dom", None),
        ),
        out_specs=(P(("dom", "tile"), None), P(("dom", "tile"))),
        check_vma=False,
    )
```

time: 207 us -> 37.2 us (0.18)
  waiting for transfers between devices: 93.2 us -> 0 us
  matrix products: 39.6 us -> 0 us
  Pallas kernels: 0 us -> 33.5 us
  starting transfers between devices: 22.9 us -> 0 us
  between operations: 19.1 us -> 0.72 us
  other arithmetic: 14.2 us -> 0 us
  blocking collectives: 11.9 us -> 0 us
  local copies, waits for them, and re-layouts: 4.79 us -> 2.47 us
    reduce_scatter x4 -> x0, waiting for transfers between devices: 61.9 us -> none  [the longest x2 39.3 us: shards(): lax.psum_scatter(partner_acc, 'tile', scatter_dimension=0, tiled=True)]
    dot_general x84 -> x0, matrix products: 39.6 us -> none  [the longest x12 10.2 us: turn(): jnp.einsum('gjr,gjd->rd', pick_right.astype(jnp.float32), grad_right, pre...]
    pallas_call x0 -> x1, Pallas kernels: none -> 33.5 us  [call(): pl.pallas_call(functools.partial(kernel, direct0, n_dom, n_tile, senders,...]
    ppermute x12 -> x0, waiting for transfers between devices: 31.3 us -> none  [from_partner(): return lax.ppermute(block, axis, route)]
    ppermute x12 -> x0, starting transfers between devices: 22.7 us -> none  [from_partner(): return lax.ppermute(block, axis, route)]
    all_gather x2 -> x0, blocking collectives: 11.9 us -> none  [shards(): own_block = lax.all_gather(low, 'tile', axis=0, tiled=True)]
    lt x12 -> x0, other arithmetic: 7.84 us -> none  [turn(): active = first + jnp.arange(TURN_TILES, dtype=jnp.int32) < live]
  transfers between devices with their start and end apart: 16 -> 0, of which waited for: 13 -> 0; matrix products, arithmetic and copies ran while one was open for 1% -> 0% of each run, Pallas kernels for 0% -> 0%
where the time goes in v1:
time: 37.2 us; the launch traced here: 36.7 us
  Pallas kernels  33.5 us (90%)
  local copies, waits for them, and re-layouts  2.47 us (7%)
  between operations  0.72 us (2%)
    pallas_call x1, Pallas kernels, call(): pl.pallas_call(functools.partial(kernel, direct0, n_dom, n_tile, senders,...  33.5 us
    unnamed x10, local copies, waits for them, and re-layouts  2.47 us

profile of v1, /device:TPU:0, one launch (start us, length us, event | category | flops | bytes accessed | tf_op | source)
XLA Modules:
  0.0 36.7 jit_solution(8796520537572270442)
XLA Ops:
  0.6 0.0 copy-start.1
  0.6 0.6 %copy-done.1 = s32[2]{0:T(128)S(1)} copy-done((s32[2]{0:T(128)S(1)}, s32[2]{0:T(128)}, u32[]{:S(2)}) %copy-start.1) | copy-done | bytes 32
  1.3 0.0 copy-start.3
  1.3 0.0 copy-start
  1.4 0.0 copy-start.2
  1.4 0.6 %copy-done.3 = f32[64]{0:T(128)S(1)} copy-done((f32[64]{0:T(128)S(1)}, f32[64]{0:T(128)}, u32[]{:S(2)}) %copy-start.3) | copy-done | bytes 280
  2.0 0.0 copy-done
  2.0 0.0 copy-done.2
  2.0 33.5 %conditional.1 = (f32[64,256]{1,0:T(8,128)S(1)}, f32[64]{0:T(128)S(1)}) conditional(s32[]{:T(128)} %bitcast.2, (s32[2]{0:T(128)S(1)}, s32[2]{0:T(128)S(1)}, s32[2,24]{1,0:T(2,128)S(1)}, f32[64,256]{1,0:T(8,128)}, f32[1,64]{1,0:T(1,128)S(1)}, /*index=5*/s32[2,24,128]{2,1,0:T(8,128)}, s32[2,24,128]{2,1,0:T(8,128)}) %tuple.34, (s32[2]{0:T(128)S(1)}, ...), branch_computations={%region_0.0_spmd, %region_1.0_spmd} | conditional | bytes 16 | solution.py:320
  2.0 33.5 %branch_0_fun.1 = (f32[64,256]{1,0:T(8,128)S(1)}, f32[1,64]{1,0:T(1,128)S(1)}) custom-call(s32[2]{0:T(128)S(1)} %get-tuple-element.33.refs_0_, s32[2]{0:T(128)S(1)} %get-tuple-element.34.refs_1_, s32[2,24]{1,0:T(2,128)S(1)} %get-tuple-element.35.refs_2_, f32[64,256]{1,0:T(8,128)} %get-tuple-element.36.refs_3_, f32[1,64]{1,0:T(1,128)S(1)} %get-tuple-element.37.refs_4_, ...), custom_call_target="tpu_custom_call" | custom-call | tf_op jit(solution)/shard_map/cond/branch_0_fun/pallas_call | solution.py:293
  35.5 0.6 %copy.17 = f32[64,256]{1,0:T(8,128)} copy(f32[64,256]{1,0:T(8,128)S(1)} %get-tuple-element.60) | data formatting | bytes 131072
  36.1 0.5 %copy.18 = f32[64]{0:T(128)} copy(f32[64]{0:T(128)S(1)} %get-tuple-element.61) | data formatting | bytes 512
Async XLA Ops:
  0.6 0.7 %copy-start.1 = (s32[2]{0:T(128)S(1)}, s32[2]{0:T(128)}, u32[]{:S(2)}) copy-start(s32[2]{0:T(128)} %param.11) | copy-start | bytes 28
  1.3 0.7 %copy-start.3 = (f32[64]{0:T(128)S(1)}, f32[64]{0:T(128)}, u32[]{:S(2)}) copy-start(f32[64]{0:T(128)} %param.10) | copy-start | bytes 772
  1.3 0.7 %copy-start = (s32[1,2,24]{2,1,0:T(2,128)S(1)}, s32[1,2,24]{2,1,0:T(2,128)}, u32[]{:S(2)}) copy-start(s32[1,2,24]{2,1,0:T(2,128)} %param.14) | copy-start | bytes 580
  1.4 0.7 %copy-start.2 = (s32[1,2]{1,0:T(1,128)S(1)}, s32[1,2]{1,0:T(1,128)}, u32[]{:S(2)}) copy-start(s32[1,2]{1,0:T(1,128)} %param.15) | copy-start | bytes 28
